TPU v7x, 32 devices: a whole 2x2x4 slice. The times are simulated.
32 devices in a mesh: grp: 2 (over x), ctx: 16 (over z, y, core).
Axes of the slice: x: 2, y: 2, z: 4, core: 2. Of those that a mesh axis runs over, the one named last changes fastest.
Arguments:
- query: bfloat16 [16384, 2048], P(('grp', 'ctx')), parts along dimension 0, may hold values from -6 to 6
- key: bfloat16 [16384, 2048], P(('grp', 'ctx')), parts along dimension 0, may hold values from -6 to 6
- value: bfloat16 [16384, 2048], P(('grp', 'ctx')), parts along dimension 0, may hold values from -6 to 6
- doc_ids: int32 [16384], P(('grp', 'ctx')), parts along dimension 0, may hold values from 0 to 7, never falling along the last dimension, each value on 1 to 4096 neighbouring positions
- gates: bfloat16 [16384, 256], P(('grp', 'ctx')), parts along dimension 0, may hold values from 0.049804688 to 1
- gain: float32 [2048], replicated, may hold values from 0.5 to 1.5
Outputs:
- mixed: bfloat16 [16384, 2048], P(('grp', 'ctx')), parts along dimension 0
There are 2 independent parts, one for each index of `grp`. A program takes and returns all parts, laid end to end along the dimension named above; an argument that names none is the same for every part. Nothing has to cross between parts.
Inputs may be any that keep to these rules, and one draw needn't show every extreme that they name: `doc_ids`: document ids never fall along the window, every id from 0 to 7 occurs, and one document covers 8192 // 2 positions.
All inputs are finite; a program needn't handle non-finite values.
Results may differ from a plain program's by a relative error of at most 0.0045.
Values may be sent and summed in bfloat16 or wider, within the bound.
A program may use at most 128 MiB of HBM per device.

v0:
```python
import jax
import jax.numpy as jnp
from jax import lax
from jax.sharding import PartitionSpec as P

H = 16
DK = 128
LEVELS = 16


def partner(value, axis, bit):
    mask = 2**bit
    pairs = [(source, source ^ mask) for source in range(lax.axis_size(axis))]
    return lax.ppermute(value, axis, pairs)


def bit_levels(count):
    places = jnp.arange(count, dtype=jnp.int32)
    mixed_bits = places[:, None] ^ places[None, :]
    levels = jnp.zeros((count, count), jnp.int32)
    for power in range(count.bit_length()):
        levels = levels + (mixed_bits >= 1 << power).astype(jnp.int32)
    return levels


def local_mix(query, key, value, doc_ids, gates):
    rows = query.shape[0]
    used = rows.bit_length()
    q_heads = query.reshape(rows, H, DK)
    k_heads = key.reshape(rows, H, DK)
    v_heads = value.reshape(rows, H, DK)
    scores = jnp.einsum("thd,shd->hts", q_heads, k_heads, preferred_element_type=jnp.float32)
    levels = bit_levels(rows)
    onehot = (levels[:, :, None] == jnp.arange(used, dtype=jnp.int32)[None, None, :]).astype(
        jnp.bfloat16
    )
    table = gates.reshape(rows, LEVELS, H)[:, :used, :]
    factor = jnp.einsum("tsl,tlh->hts", onehot, table, preferred_element_type=jnp.float32)
    scale = jnp.exp2(-0.5 * levels.astype(jnp.float32))
    places = jnp.arange(rows, dtype=jnp.int32)
    allowed = (places[None, :] <= places[:, None]) & (doc_ids[None, :] == doc_ids[:, None])
    weighted = jnp.where(allowed[None], scores * factor * scale[None], 0.0).astype(jnp.bfloat16)
    return jnp.einsum("hts,shd->thd", weighted, v_heads, preferred_element_type=jnp.float32)


def run_summary(key, value, doc_ids):
    rows = key.shape[0]
    first_id = doc_ids[0]
    last_id = doc_ids[rows - 1]
    keep = doc_ids == last_id
    kept = jnp.where(keep[:, None], key, jnp.zeros_like(key))
    state = jnp.einsum(
        "thd,the->hde",
        kept.reshape(rows, H, DK),
        value.reshape(rows, H, DK),
        preferred_element_type=jnp.float32,
    )
    meta = jnp.stack([first_id, last_id, (first_id == last_id).astype(jnp.int32)])
    return (state, meta)


def apply_level(bit, power, mine, other, q_float, doc_ids, gates, far):
    state, meta = mine
    other_state, other_meta = other
    upper = lax.axis_index("ctx") >> bit & 1 == 1
    level = power + bit + 1
    valid = (doc_ids == other_meta[1]) & upper
    weight = gates[:, level * H : (level + 1) * H].astype(jnp.float32) * 2.0 ** (-0.5 * level)
    weight = jnp.where(valid[:, None], weight, 0.0)
    term = jnp.einsum("thd,hde->the", q_float, other_state, precision=lax.Precision.HIGHEST)
    far = far + weight[:, :, None] * term
    low_state = jnp.where(upper, other_state, state)
    high_state = jnp.where(upper, state, other_state)
    low_meta = jnp.where(upper, other_meta, meta)
    high_meta = jnp.where(upper, meta, other_meta)
    joins = (high_meta[2] == 1) & (high_meta[0] == low_meta[1])
    merged = high_state + jnp.where(joins, low_state, 0.0)
    single = ((low_meta[2] == 1) & joins).astype(jnp.int32)
    return (far, (merged, jnp.stack([low_meta[0], high_meta[1], single])))


def body(query, key, value, doc_ids, gates, gain):
    rows = query.shape[0]
    power = rows.bit_length() - 1
    log_ctx = lax.axis_size("ctx").bit_length() - 1
    mine = run_summary(key, value, doc_ids)
    their_keys, their_values, their_ids = partner((key, value, doc_ids), "ctx", 0)
    other = run_summary(their_keys, their_values, their_ids)
    near = local_mix(query, key, value, doc_ids, gates)
    q_float = query.reshape(rows, H, DK).astype(jnp.float32)
    far = jnp.zeros((rows, H, DK), jnp.float32)
    far, mine = apply_level(0, power, mine, other, q_float, doc_ids, gates, far)
    for bit in range(1, log_ctx):
        other = partner((mine[0], mine[1]), "ctx", bit)
        far, mine = apply_level(bit, power, mine, other, q_float, doc_ids, gates, far)
    attended = near + far
    mean_square = jnp.mean(attended * attended, axis=-1, keepdims=True)
    normed = attended * lax.rsqrt(mean_square + 1e-06) * gain.reshape(H, DK)
    return normed.reshape(rows, H * DK).astype(jnp.bfloat16)


def solution(mesh):
    placed = (
        P(("grp", "ctx"), None),
        P(("grp", "ctx"), None),
        P(("grp", "ctx"), None),
        P(("grp", "ctx")),
        P(("grp", "ctx"), None),
        P(),
    )
    return jax.shard_map(
        body, mesh=mesh, in_specs=placed, out_specs=P(("grp", "ctx"), None), check_vma=False
    )
```

profile of v0, /device:TPU:0, one launch (start us, length us, event | category | flops | bytes accessed | tf_op | source)
XLA Modules:
  0.0 181.0 jit_solution(14194435342632761414)
XLA Ops:
  0.5 4.0 %copy.52 = bf16[512,2048]{0,1:T(8,128)(2,1)} copy(bf16[512,2048]{1,0:T(8,128)(2,1)} %param.8) | data formatting | bytes 4194304 | tf_op args[2]
  5.3 2.9 %iota_compare_fusion = pred[512,512,10]{1,0,2:T(32,128)(4,1)} fusion(s32[512,512]{1,0:T(8,128)S(1)} %convert_add_fusion), kind=kLoop, calls=%fused_computation.6 | loop fusion | flops 2621440 | bytes 3670016 | tf_op jit(solution)/shard_map/eq | solution.py:34
  12.0 2.6 %broadcast_select_fusion.6 = (s32[3]{0:T(128)S(1)}, s32[3]{0:T(128)S(1)}) fusion(pred[]{:T(512)S(6)} %eq.132, s32[1]{0:T(128)} %bitcast.11, s32[1]{0:T(128)} %get-tuple-element.17, s32[1]{0:T(128)} %get-tuple-element.16, s32[1]{0:T(128)} %bitcast.8, s32[1]{0:T(128)} %get-tuple-element.15, s32[1]{0:T(128)} %get-tuple-element.14), kind=kLoop, calls=%fused_computation.73 | loop fusion | flops 18 | bytes 49 | tf_op jit(solution)/shard_map/jit(_where)/select_n | solution.py:75
  18.4 1.3 pad_add_fusion.2
  19.8 2.5 %collective-permute-start.3 = (s32[3]{0:T(128)S(1)}, s32[3]{0:T(128)S(1)}, u32[]{:S(2)}, u32[]{:S(2)}) collective-permute-start(s32[3]{0:T(128)S(1)} %pad_add_fusion.2), channel_id=1, source_target_pairs={{0,2},{1,3},{2,0},{3,1},{4,6},{5,7},{6,4},{7,5},{8,10},{9,11},{10,... | collective-permute-start | bytes 44 | tf_op jit(solution)/shard_map/ppermute | solution.py:14
  23.8 1.3 broadcast_select_fusion.5
  30.2 2.1 %collective-permute-start.5 = (s32[3]{0:T(128)S(1)}, s32[3]{0:T(128)S(1)}, u32[]{:S(2)}, u32[]{:S(2)}) collective-permute-start(s32[3]{0:T(128)S(1)} %pad_add_fusion.3), channel_id=1, source_target_pairs={{0,4},{1,5},{2,6},{3,7},{4,0},{5,1},{6,2},{7,3},{8,12},{9,13},{10,... | collective-permute-start | bytes 44 | tf_op jit(solution)/shard_map/ppermute | solution.py:14
  40.1 3.0 %collective-permute-start.7 = (s32[3]{0:T(128)S(1)}, s32[3]{0:T(128)S(1)}, u32[]{:S(2)}, u32[]{:S(2)}) collective-permute-start(s32[3]{0:T(128)S(1)} %pad_add_fusion.4), channel_id=1, source_target_pairs={{0,8},{1,9},{2,10},{3,11},{4,12},{5,13},{6,14},{7,15},{8,0},{9,1},... | collective-permute-start | bytes 44 | tf_op jit(solution)/shard_map/ppermute | solution.py:14
  45.2 3.1 %compare_and_fusion.3 = (pred[512]{0:T(512)(128)(4,1)S(1)}, pred[512]{0:T(512)(128)(4,1)S(1)}, pred[512]{0:T(512)(128)(4,1)S(1)}, pred[512]{0:T(512)(128)(4,1)S(1)}, pred[512]{0:T(512)(128)(4,1)S(1)}) fusion(s32[512]{0:T(512)S(1)} %copy-done.5, s32[]{:T(128)} %bitcast.3, pred[]{:T(512)S(6)} %eq.132, pred[]{:T(512)S(6)} %eq.142, s32[]{:T(128)} %bitcast.15, ...), kind=kLoop, calls=%fused_computation.66 | loop fusion | flops 4608 | bytes 4632 | tf_op jit(solution)/shard_map/and | solution.py:67
  48.3 3.1 %broadcast_select_fusion = bf16[512,2048]{1,0:T(8,128)(2,1)} fusion(bf16[512,2048]{1,0:T(8,128)(2,1)} %param.7, pred[512]{0:T(512)(128)(4,1)S(1)} %get-tuple-element.11), kind=kLoop, calls=%fused_computation.31 | loop fusion | flops 1048576 | bytes 4194816 | tf_op jit(solution)/shard_map/jit(_where)/select_n | solution.py:51
  51.4 4.0 %copy.75 = bf16[512,2048]{0,1:T(8,128)(2,1)} copy(bf16[512,2048]{1,0:T(8,128)(2,1)} %broadcast_select_fusion) | data formatting | bytes 4194304 | tf_op jit(solution)/shard_map/reshape | solution.py:54
  55.4 3.1 %broadcast_select_fusion.1 = bf16[512,2048]{1,0:T(8,128)(2,1)} fusion(bf16[512,2048]{1,0:T(8,128)(2,1)} %collective-permute-done.1, pred[512]{0:T(512)(128)(4,1)S(1)} %broadcast_compare_fusion.1), kind=kLoop, calls=%fused_computation.32 | loop fusion | flops 1048576 | bytes 4194816 | tf_op jit(solution)/shard_map/jit(_where)/select_n | solution.py:51
  58.5 3.9 %copy.74 = bf16[512,2048]{0,1:T(8,128)(2,1)} copy(bf16[512,2048]{1,0:T(8,128)(2,1)} %broadcast_select_fusion.1) | data formatting | bytes 4194304 | tf_op jit(solution)/shard_map/reshape | solution.py:54
  62.5 3.1 %fusion.57 = f32[16,128,128]{2,1,0:T(8,128)S(1)} fusion(bf16[512,16,128]{0,2,1:T(8,128)(2,1)} %bitcast.122, bf16[512,16,128]{0,2,1:T(8,128)(2,1)} %bitcast.5), kind=kOutput, calls=%fused_computation.89 | convolution fusion | flops 268435456 | bytes 5242880 | tf_op jit(solution)/shard_map/thd,the->hde/dot_general | solution.py:52
  66.0 1.7 select_add_fusion.2
  67.7 1.8 %collective-permute-start.4 = (f32[16,128,128]{2,1,0:T(8,128)}, f32[16,128,128]{2,1,0:T(8,128)}, u32[]{:S(2)}, u32[]{:S(2)}) collective-permute-start(f32[16,128,128]{2,1,0:T(8,128)} %select_add_fusion.2), channel_id=1, source_target_pairs={{0,2},{1,3},{2,0},{3,1},{4,6},{5,7},{6,4},{7,5},{8,10},{9,11},{10,... | collective-permute-start | bytes 3145736 | tf_op jit(solution)/shard_map/ppermute | solution.py:14
  71.7 1.6 slice.120
  73.2 3.8 %copy.76 = bf16[512,10,16]{1,2,0:T(8,128)(2,1)} copy(bf16[512,10,16]{0,2,1:T(8,128)(2,1)} %slice.120) | data formatting | bytes 327680
  77.9 13.0 %fusion.3 = f32[512,512,16]{1,2,0:T(8,128)} fusion(bf16[512,10,16]{1,2,0:T(8,128)(2,1)} %copy.76, pred[512,512,10]{1,0,2:T(32,128)(4,1)} %iota_compare_fusion), kind=kOutput, calls=%fused_computation.4 | convolution fusion | flops 83886080 | bytes 19562496 | tf_op jit(solution)/shard_map/tsl,tlh->hts/dot_general | solution.py:38
  90.9 2.7 %select_add_fusion.1 = f32[16,128,128]{2,1,0:T(8,128)} fusion(f32[16,128,128]{2,1,0:T(8,128)} %collective-permute-done.4, f32[16,128,128]{2,1,0:T(8,128)} %select_add_fusion.2, pred[]{:T(512)} %bitcast.19, pred[]{:T(512)S(6)} %eq.142), kind=kLoop, calls=%fused_computation.41 | loop fusion | flops 1048576 | bytes 3145730 | tf_op jit(solution)/shard_map/add | solution.py:77
  93.6 1.6 collective-permute-start.6
  95.2 22.7 %fusion.9 = f32[16,512,128]{1,2,0:T(8,128)} fusion(f32[512,512,16]{1,2,0:T(8,128)} %fusion.3, f32[512,512]{1,0:T(8,128)} %multiply_exponential_fusion, pred[512,512]{1,0:T(8,128)(4,1)} %fusion.47, bf16[512,2048]{1,0:T(8,128)(2,1)} %param.8, bf16[512,2048]{1,0:T(8,128)(2,1)} %param.7, bf16[512,2048]{1,0:T(8,128)(2,1)S(1)} %copy-done), kind=kOutput, calls=%fused_computation.17 | convolution fusion | flops 2164260864 | bytes 28573696 | tf_op jit(solution)/shard_map/hts,shd->thd/dot_general | solution.py:43
  117.9 1.5 multiply_select_fusion.3
  123.6 1.7 select_add_fusion
  125.3 2.6 %collective-permute-start.8 = (f32[16,128,128]{2,1,0:T(8,128)S(1)}, f32[16,128,128]{2,1,0:T(8,128)}, u32[]{:S(2)}, u32[]{:S(2)}) collective-permute-start(f32[16,128,128]{2,1,0:T(8,128)S(1)} %select_add_fusion), channel_id=1, source_target_pairs={{0,8},{1,9},{2,10},{3,11},{4,12},{5,13},{6,14},{7,15},{8,0},{9,1},... | collective-permute-start | bytes 3145736 | tf_op jit(solution)/shard_map/ppermute | solution.py:14
  128.0 2.0 %fusion.20 = f32[16,128,512]{2,1,0:T(8,128)S(1)} fusion(f32[16,128,128]{2,1,0:T(8,128)S(1)} %fusion.57, bf16[512,2048]{1,0:T(8,128)(2,1)S(1)} %copy-done), kind=kOutput, calls=%fused_computation.28 | convolution fusion | flops 1610612736 | bytes 7340032 | tf_op jit(solution)/shard_map/thd,hde->the/dot_general | solution.py:70
  130.0 3.3 %fusion.18 = f32[16,128,512]{2,1,0:T(8,128)S(1)} fusion(f32[16,128,128]{2,1,0:T(8,128)} %collective-permute-done.4, bf16[512,2048]{1,0:T(8,128)(2,1)S(1)} %copy-done), kind=kOutput, calls=%fused_computation.26 | convolution fusion | flops 1610612736 | bytes 7340032 | tf_op jit(solution)/shard_map/thd,hde->the/dot_general | solution.py:70
  133.3 3.4 %fusion.16 = f32[16,128,512]{2,1,0:T(8,128)S(1)} fusion(f32[16,128,128]{2,1,0:T(8,128)} %collective-permute-done.6, bf16[512,2048]{1,0:T(8,128)(2,1)S(1)} %copy-done), kind=kOutput, calls=%fused_computation.24 | convolution fusion | flops 1610612736 | bytes 7340032 | tf_op jit(solution)/shard_map/thd,hde->the/dot_general | solution.py:70
  136.7 33.7 %collective-permute-done.8 = f32[16,128,128]{2,1,0:T(8,128)} collective-permute-done((f32[16,128,128]{2,1,0:T(8,128)S(1)}, f32[16,128,128]{2,1,0:T(8,128)}, u32[]{:S(2)}, u32[]{:S(2)}) %collective-permute-start.8) | collective-permute-done | bytes 1048608 | tf_op jit(solution)/shard_map/ppermute | solution.py:14
  170.4 4.7 %multiply_reduce_fusion = (f32[512,16]{0,1:T(8,128)S(1)}, f32[512,16,128]{0,2,1:T(8,128)S(1)}) fusion(f32[16,128,128]{2,1,0:T(8,128)} %collective-permute-done.8, f32[512,16]{0,1:T(8,128)S(1)} %copy.65, f32[16,128,512]{2,1,0:T(8,128)S(1)} %fusion.16, f32[512,16]{0,1:T(8,128)S(1)} %copy.62, f32[16,128,512]{2,1,0:T(8,128)S(1)} %fusion.18, ...), kind=kOutput, calls=%fused_computation.16 | convolution fusion | flops 1621090304 | bytes 24281088 | tf_op jit(solution)/shard_map/thd,hde->the/dot_general | solution.py:70
  175.2 2.0 %multiply_convert_fusion = bf16[512,16,128]{0,2,1:T(8,128)(2,1)} fusion(f32[512,16,128]{0,2,1:T(8,128)S(1)} %get-tuple-element.41, f32[16,128]{1,0:T(8,128)S(1)} %bitcast.126, f32[512,16]{0,1:T(8,128)S(1)} %add_rsqrt_fusion), kind=kLoop, calls=%fused_computation.15 | loop fusion | flops 3145728 | bytes 6332416 | tf_op jit(solution)/shard_map/convert_element_type | solution.py:99
  177.1 3.9 %copy.68 = bf16[512,2048]{1,0:T(8,128)(2,1)} copy(bf16[512,2048]{0,1:T(8,128)(2,1)} %bitcast.123) | data formatting | bytes 4194304 | tf_op jit(solution)/shard_map/convert_element_type | solution.py:99
  (49 shorter events, 22.9 us)
Async XLA Ops:
  0.0 95.2 %copy-start = (bf16[512,2048]{1,0:T(8,128)(2,1)S(1)}, bf16[512,2048]{1,0:T(8,128)(2,1)}, u32[]{:S(2)}) copy-start(bf16[512,2048]{1,0:T(8,128)(2,1)} %param.6) | copy-start | bytes 6291460
  0.0 10.0 %collective-permute-start = (s32[512]{0:T(512)}, s32[512]{0:T(512)S(1)}, u32[]{:S(2)}, u32[]{:S(2)}) collective-permute-start(s32[512]{0:T(512)} %param.9), channel_id=1, source_target_pairs={{0,1},{1,0},{2,3},{3,2},{4,5},{5,4},{6,7},{7,6},{8,9},{9,8},{10,11... | collective-permute-start | bytes 6152 | tf_op jit(solution)/shard_map/ppermute | solution.py:14
  0.5 55.0 %collective-permute-start.1 = (bf16[512,2048]{1,0:T(8,128)(2,1)}, bf16[512,2048]{1,0:T(8,128)(2,1)}, u32[]{:S(2)}, u32[]{:S(2)}) collective-permute-start(bf16[512,2048]{1,0:T(8,128)(2,1)} %param.7), channel_id=1, source_target_pairs={{0,1},{1,0},{2,3},{3,2},{4,5},{5,4},{6,7},{7,6},{8,9},{9,8},{10,11... | collective-permute-start | bytes 6291464 | tf_op jit(solution)/shard_map/ppermute | solution.py:14
  4.5 57.9 %collective-permute-start.2 = (bf16[512,2048]{0,1:T(8,128)(2,1)}, bf16[512,2048]{0,1:T(8,128)(2,1)}, u32[]{:S(2)}, u32[]{:S(2)}) collective-permute-start(bf16[512,2048]{0,1:T(8,128)(2,1)} %copy.52), channel_id=1, source_target_pairs={{0,1},{1,0},{2,3},{3,2},{4,5},{5,4},{6,7},{7,6},{8,9},{9,8},{10,11... | collective-permute-start | bytes 6291464 | tf_op jit(solution)/shard_map/ppermute | solution.py:14
  5.3 2.9 %copy-start.5 = (s32[512]{0:T(512)S(1)}, s32[512]{0:T(512)}, u32[]{:S(2)}) copy-start(s32[512]{0:T(512)} %param.9) | copy-start | bytes 6148
  19.8 4.0 %collective-permute-start.3 = (s32[3]{0:T(128)S(1)}, s32[3]{0:T(128)S(1)}, u32[]{:S(2)}, u32[]{:S(2)}) collective-permute-start(s32[3]{0:T(128)S(1)} %pad_add_fusion.2), channel_id=1, source_target_pairs={{0,2},{1,3},{2,0},{3,1},{4,6},{5,7},{6,4},{7,5},{8,10},{9,11},{10,... | collective-permute-start | bytes 44 | tf_op jit(solution)/shard_map/ppermute | solution.py:14
  30.2 3.6 %collective-permute-start.5 = (s32[3]{0:T(128)S(1)}, s32[3]{0:T(128)S(1)}, u32[]{:S(2)}, u32[]{:S(2)}) collective-permute-start(s32[3]{0:T(128)S(1)} %pad_add_fusion.3), channel_id=1, source_target_pairs={{0,4},{1,5},{2,6},{3,7},{4,0},{5,1},{6,2},{7,3},{8,12},{9,13},{10,... | collective-permute-start | bytes 44 | tf_op jit(solution)/shard_map/ppermute | solution.py:14
  40.1 4.6 %collective-permute-start.7 = (s32[3]{0:T(128)S(1)}, s32[3]{0:T(128)S(1)}, u32[]{:S(2)}, u32[]{:S(2)}) collective-permute-start(s32[3]{0:T(128)S(1)} %pad_add_fusion.4), channel_id=1, source_target_pairs={{0,8},{1,9},{2,10},{3,11},{4,12},{5,13},{6,14},{7,15},{8,0},{9,1},... | collective-permute-start | bytes 44 | tf_op jit(solution)/shard_map/ppermute | solution.py:14
  62.5 3.1 %copy-start.3 = (bf16[512,2048]{1,0:T(8,128)(2,1)S(1)}, bf16[512,2048]{1,0:T(8,128)(2,1)}, u32[]{:S(2)}) copy-start(bf16[512,2048]{1,0:T(8,128)(2,1)} %param.8) | copy-start | bytes 6291460
  62.5 3.5 %copy-start.4 = (bf16[512,2048]{0,1:T(8,128)(2,1)S(1)}, bf16[512,2048]{0,1:T(8,128)(2,1)}, u32[]{:S(2)}) copy-start(bf16[512,2048]{0,1:T(8,128)(2,1)} %copy.75) | copy-start | bytes 6291460
  66.0 4.9 %copy-start.2 = (bf16[512,256]{1,0:T(8,128)(2,1)S(1)}, bf16[512,256]{1,0:T(8,128)(2,1)}, u32[]{:S(2)}) copy-start(bf16[512,256]{1,0:T(8,128)(2,1)} %param.10) | copy-start | bytes 786436
  67.7 23.3 %collective-permute-start.4 = (f32[16,128,128]{2,1,0:T(8,128)}, f32[16,128,128]{2,1,0:T(8,128)}, u32[]{:S(2)}, u32[]{:S(2)}) collective-permute-start(f32[16,128,128]{2,1,0:T(8,128)} %select_add_fusion.2), channel_id=1, source_target_pairs={{0,2},{1,3},{2,0},{3,1},{4,6},{5,7},{6,4},{7,5},{8,10},{9,11},{10,... | collective-permute-start | bytes 3145736 | tf_op jit(solution)/shard_map/ppermute | solution.py:14
  93.6 30.0 %collective-permute-start.6 = (f32[16,128,128]{2,1,0:T(8,128)}, f32[16,128,128]{2,1,0:T(8,128)}, u32[]{:S(2)}, u32[]{:S(2)}) collective-permute-start(f32[16,128,128]{2,1,0:T(8,128)} %select_add_fusion.1), channel_id=1, source_target_pairs={{0,4},{1,5},{2,6},{3,7},{4,0},{5,1},{6,2},{7,3},{8,12},{9,13},{10,... | collective-permute-start | bytes 3145736 | tf_op jit(solution)/shard_map/ppermute | solution.py:14
  125.3 45.1 %collective-permute-start.8 = (f32[16,128,128]{2,1,0:T(8,128)S(1)}, f32[16,128,128]{2,1,0:T(8,128)}, u32[]{:S(2)}, u32[]{:S(2)}) collective-permute-start(f32[16,128,128]{2,1,0:T(8,128)S(1)} %select_add_fusion), channel_id=1, source_target_pairs={{0,8},{1,9},{2,10},{3,11},{4,12},{5,13},{6,14},{7,15},{8,0},{9,1},... | collective-permute-start | bytes 3145736 | tf_op jit(solution)/shard_map/ppermute | solution.py:14
  133.3 37.1 %copy-start.1 = (f32[16,512,128]{1,2,0:T(8,128)S(1)}, f32[16,512,128]{1,2,0:T(8,128)}, u32[]{:S(2)}) copy-start(f32[16,512,128]{1,2,0:T(8,128)} %fusion.9) | copy-start | bytes 12582916
  136.7 38.4 %copy-start.6 = (f32[2048]{0:T(1024)S(1)}, f32[2048]{0:T(1024)}, u32[]{:S(2)}) copy-start(f32[2048]{0:T(1024)} %param.11) | copy-start | bytes 24580
where the time goes:
time: 182 us; the launch traced here: 181 us
  matrix products  53.9 us (30%)
  waiting for transfers between devices  36.4 us (20%)
  local copies, waits for them, and re-layouts  33.4 us (18%)
  other arithmetic  32.4 us (18%)
  starting transfers between devices  14.7 us (8%)
  between operations  10.2 us (6%)
    ppermute x9, waiting for transfers between devices, partner(): return lax.ppermute(value, axis, pairs)  36.4 us
    dot_general x1, matrix products, local_mix(): jnp.einsum('hts,shd->thd', weighted, v_heads, preferred_element_type=jnp....  22.7 us
    ppermute x9, starting transfers between devices, partner(): return lax.ppermute(value, axis, pairs)  14.7 us
    dot_general x4, matrix products, apply_level(): jnp.einsum('thd,hde->the', q_float, other_state, precision=lax.Precision....  13.4 us
    dot_general x1, matrix products, local_mix(): jnp.einsum('tsl,tlh->hts', onehot, table, preferred_element_type=jnp.floa...  13 us
    unnamed x17, local copies, waits for them, and re-layouts  9.06 us
    reshape x2, local copies, waits for them, and re-layouts, run_summary(): kept.reshape(rows, H, DK)  7.89 us
    select_n x2, other arithmetic, run_summary(): kept = jnp.where(keep[:, None], key, jnp.zeros_like(key))  6.24 us
  transfers between devices with their start and end apart: 9, of which 4 were waited for; matrix products, arithmetic and copies ran while one was open for 55% of the time, Pallas kernels for 0%

commit v1 on v0

v1 whole, which is shorter than its diff:
```python
import functools
import math

import jax
import jax.numpy as jnp
from jax import lax
from jax.experimental import pallas as pl
from jax.experimental.pallas import tpu as pltpu
from jax.sharding import PartitionSpec as P

H = 16
DK = 128
LEVELS = 16
T = 128
HC = 2
NC = H // HC
HALF = NC // 2
CW = HC * DK
SR = CW + 16
F32 = jnp.float32
BF16 = jnp.bfloat16
R2 = 2.0**-0.5
MESH = pl.DeviceIdType.MESH


def kernel(n, q_hbm, k_hbm, v_hbm, doc_ref, g_ref, gain_ref, out_hbm,
           q, k, v, ost, acc, glo, gm, doct, smask, kmask, loc, mine, sbuf, rbuf,
           ksem, vsem, qsem, osem, send_sem, recv_sem, fwd_sem):
    nb = n.bit_length() - 1
    rows = q.shape[0]
    tiles = rows // T
    me = lax.axis_index("ctx")
    p = lax.rem(me, 2)
    sib = me + 1 - 2 * p

    def partner(b):
        bit = lax.rem(lax.div(me, 2**b), 2)
        return me + (1 - 2 * bit) * 2**b

    def upper(b):
        return lax.rem(lax.div(me, 2**b), 2) == 1

    def cols(c):
        return pl.ds(pl.multiple_of(c * CW, CW), CW)

    def hcols(h):
        return pl.ds(pl.multiple_of(h * DK, DK), DK)

    def load(src, dst, sem, c):
        return pltpu.make_async_copy(src.at[:, cols(c)], dst.at[:, cols(c)], sem.at[c])

    def order(i):
        return lax.rem(lax.div(i, HALF) + 1 - p, 2) * HALF + lax.rem(i, HALF)

    @pl.loop(0, NC)
    def _(i):
        load(k_hbm, k, ksem, order(i)).start()
        load(v_hbm, v, vsem, order(i)).start()

    @pl.loop(0, NC)
    def _(i):
        load(q_hbm, q, qsem, order(i)).start()

    barrier = pltpu.get_barrier_semaphore()
    for b in range(nb):
        pl.semaphore_signal(barrier, inc=1, device_id={"ctx": partner(b)}, device_id_type=MESH)

    it = lax.broadcasted_iota(jnp.int32, (T, T), 0)
    js = lax.broadcasted_iota(jnp.int32, (T, T), 1)
    xo = jnp.bitwise_xor(it, js)
    lev = jnp.zeros((T, T), jnp.int32)
    for power in range(7):
        lev = lev + (xo >= 2**power).astype(jnp.int32)
    scale = jnp.exp2(lev.astype(F32) * -0.5)
    firsts, lasts = [], []
    for j in range(tiles):
        rs = slice(j * T, (j + 1) * T)
        drow = jnp.broadcast_to(doc_ref[j : j + 1, :].astype(F32), (T, T))
        dt = drow.T
        doct[rs, :] = dt
        first, last = dt[0:1, :], dt[T - 1 : T, :]
        firsts.append(first)
        lasts.append(last)
        smask[rs, :] = jnp.where((dt == drow) & (js <= it), scale, 0.0)
        kmask[rs, :] = jnp.where(dt == last, 1.0, 0.0).astype(BF16)
        glo[rs, :] = g_ref[rs, 0:128].astype(F32)
        ghi = g_ref[rs, 128:256].astype(F32)
        if j % 2 == 1:
            gm[0, rs, :] = jnp.where(dt == lasts[j - 1], ghi, 0.0)
        if j >= 2:
            gm[1, rs, :] = jnp.where(dt == lasts[1], ghi, 0.0)

    def joins(hi_first, hi_last, lo_last):
        return jnp.where((hi_first == hi_last) & (hi_first == lo_last), 1.0, 0.0)

    j01 = joins(firsts[1], lasts[1], lasts[0])
    j23 = joins(firsts[3], lasts[3], lasts[2])
    jall = joins(firsts[2], lasts[3], lasts[1])
    rowid = lax.broadcasted_iota(jnp.int32, (16, DK), 0)

    def meta(first, last):
        return jnp.where(rowid == 0, first, last).astype(BF16)

    meta0 = meta(firsts[0], lasts[3])

    pl.semaphore_wait(barrier, nb)

    def send(b, c):
        to = sib if b == 0 else partner(b)
        return pltpu.make_async_remote_copy(
            src_ref=sbuf.at[b, c], dst_ref=rbuf.at[b, c],
            send_sem=send_sem.at[b, c], recv_sem=recv_sem.at[b, c],
            device_id={"ctx": to}, device_id_type=MESH)

    def forward(b, c):
        return pltpu.make_async_remote_copy(
            src_ref=rbuf.at[b, c], dst_ref=rbuf.at[b, c],
            send_sem=fwd_sem.at[b, c], recv_sem=recv_sem.at[b, c],
            device_id={"ctx": sib}, device_id_type=MESH)

    def states(i, own):
        c = order(i)
        load(k_hbm, k, ksem, c).wait()
        load(v_hbm, v, vsem, c).wait()
        for x in range(HC):
            h = c * HC + x
            t = []
            for j in range(tiles):
                rs = slice(j * T, (j + 1) * T)
                km = k[rs, hcols(h)] * kmask[rs, :]
                t.append(lax.dot_general(km, v[rs, hcols(h)], (((0,), (0,)), ((), ())),
                                         preferred_element_type=F32))
            low = t[1] + j01 * t[0]
            high = t[3] + j23 * t[2]
            loc[0, h] = (t[0] * 2.0**-4).astype(BF16)
            loc[1, h] = (t[2] * 2.0**-4).astype(BF16)
            loc[2, h] = (low * 2.0**-4.5).astype(BF16)
            run = (high + jall * low) * 2.0**-5
            if own:
                mine[i - HALF, x * DK : (x + 1) * DK, :] = run
            sbuf[0, c, x * DK : (x + 1) * DK, :] = run.astype(BF16)
        sbuf[0, c, CW:SR, :] = meta0
        send(0, c).start()

    @pl.loop(0, HALF)
    def _(i):
        states(i, False)

    @pl.loop(HALF, NC)
    def _(i):
        states(i, True)

    def step(b, i):
        c = p * HALF + i
        send(b, c).wait_recv()
        if b >= 1:
            forward(b, c).start()
        if b < nb - 1:
            up = upper(b)
            mf = sbuf[b, c, CW:SR, :].astype(F32)
            of = rbuf[b, c, CW:SR, :].astype(F32)
            hi, lo = jnp.where(up, mf, of), jnp.where(up, of, mf)
            join = joins(hi[0:1], hi[1:2], lo[1:2])
            cm, co = jnp.where(up, 1.0, join) * R2, jnp.where(up, join, 1.0) * R2
            merged = mine[i] * cm + rbuf[b, c, 0:CW, :].astype(F32) * co
            mine[i] = merged
            sbuf[b + 1, c, 0:CW, :] = merged.astype(BF16)
            sbuf[b + 1, c, CW:SR, :] = meta(lo[0:1], hi[1:2])
            send(b + 1, c).start()

    lev16 = lev * 16

    def near(c):
        load(q_hbm, q, qsem, c).wait()
        for x in range(HC):
            h = c * HC + x
            idx = lev16 + h
            for j in range(tiles):
                rs = slice(j * T, (j + 1) * T)
                qj = q[rs, hcols(h)]
                s = lax.dot_general(qj, k[rs, hcols(h)], (((1,), (1,)), ((), ())),
                                    preferred_element_type=F32)
                f = jnp.take_along_axis(glo[rs, :], idx, axis=1)
                w = (s * f * smask[rs, :]).astype(BF16)
                o = jnp.dot(w, v[rs, hcols(h)], preferred_element_type=F32)
                if j % 2 == 1:
                    w8 = jnp.take_along_axis(gm[0, rs, :], jnp.full((T, T), h, jnp.int32), axis=1)
                    o = o + w8 * jnp.dot(qj, loc[j // 2, h], preferred_element_type=F32)
                if j >= 2:
                    w9 = jnp.take_along_axis(gm[1, rs, :], jnp.full((T, T), 16 + h, jnp.int32), axis=1)
                    o = o + w9 * jnp.dot(qj, loc[2, h], preferred_element_type=F32)
                acc[rs, hcols(h)] = o

    def weights(b):
        last = rbuf[b, p * HALF, CW:SR, :].astype(F32)[1:2]
        last = jnp.where(upper(b), last, -1.0)
        for j in range(tiles):
            rs = slice(j * T, (j + 1) * T)
            gm[b % 2, rs, :] = jnp.where(doct[rs, :] == last, g_ref[rs, 128:256].astype(F32), 0.0)

    def far(b, c, final):
        for x in range(HC):
            h = c * HC + x
            idx = jnp.full((T, T), (2 + b) * 16 + h, jnp.int32)
            st = rbuf[b, c, x * DK : (x + 1) * DK, :]
            for j in range(tiles):
                rs = slice(j * T, (j + 1) * T)
                w = jnp.take_along_axis(gm[b % 2, rs, :], idx, axis=1)
                a = acc[rs, hcols(h)] + w * jnp.dot(q[rs, hcols(h)], st, preferred_element_type=F32)
                if not final:
                    acc[rs, hcols(h)] = a
                else:
                    ms = jnp.dot((a * a).astype(BF16), jnp.full((DK, DK), 1.0 / DK, BF16),
                                 preferred_element_type=F32)
                    y = a * lax.rsqrt(ms + 1e-6) * gain_ref[:, hcols(h)]
                    ost[rs, hcols(h)] = y.astype(BF16)

    @pl.loop(0, HALF)
    def _(i):
        step(0, i)
        near(p * HALF + i)
        near((1 - p) * HALF + i)

    for b in range(1, nb):
        weights(b - 1)

        @pl.loop(0, HALF)
        def _(i):
            step(b, i)
            far(b - 1, p * HALF + i, False)
            oc = (1 - p) * HALF + i
            send(b - 1, oc).wait_recv()
            far(b - 1, oc, False)

    weights(nb - 1)

    def put(c):
        return pltpu.make_async_copy(ost.at[:, cols(c)], out_hbm.at[:, cols(c)], osem.at[c])

    @pl.loop(0, HALF)
    def _(i):
        c = p * HALF + i
        far(nb - 1, c, True)
        put(c).start()

    @pl.loop(0, HALF)
    def _(i):
        c = (1 - p) * HALF + i
        send(nb - 1, c).wait_recv()
        far(nb - 1, c, True)
        put(c).start()

    @pl.loop(0, NC)
    def _(i):
        send(0, i).wait_send()
        put(i).wait()

    for b in range(1, nb):

        @pl.loop(0, HALF)
        def _(i):
            send(b, p * HALF + i).wait_send()
            forward(b, p * HALF + i).wait_send()


def body(query, key, value, doc_ids, gates, gain):
    n = lax.axis_size("ctx")
    nb = n.bit_length() - 1
    rows, width = query.shape
    hbm = pl.BlockSpec(memory_space=pl.ANY)
    vmem = pl.BlockSpec(memory_space=pltpu.VMEM)
    dma = pltpu.SemaphoreType.DMA
    return pl.pallas_call(
        functools.partial(kernel, n),
        out_shape=jax.ShapeDtypeStruct((rows, width), BF16),
        in_specs=[hbm, hbm, hbm, vmem, vmem, vmem],
        out_specs=hbm,
        scratch_shapes=[
            pltpu.VMEM((rows, width), BF16),
            pltpu.VMEM((rows, width), BF16),
            pltpu.VMEM((rows, width), BF16),
            pltpu.VMEM((rows, width), BF16),
            pltpu.VMEM((rows, width), F32),
            pltpu.VMEM((rows, 128), F32),
            pltpu.VMEM((2, rows, 128), F32),
            pltpu.VMEM((rows, 128), F32),
            pltpu.VMEM((rows, 128), F32),
            pltpu.VMEM((rows, 128), BF16),
            pltpu.VMEM((3, H, DK, DK), BF16),
            pltpu.VMEM((HALF, CW, DK), F32),
            pltpu.VMEM((nb, NC, SR, DK), BF16),
            pltpu.VMEM((nb, NC, SR, DK), BF16),
            dma((NC,)), dma((NC,)), dma((NC,)), dma((NC,)),
            dma((nb, NC)), dma((nb, NC)), dma((nb, NC)),
        ],
        compiler_params=pltpu.CompilerParams(
            collective_id=0, has_side_effects=True, vmem_limit_bytes=56 * 2**20),
    )(query, key, value, doc_ids.reshape(rows // T, T), gates, gain.reshape(1, width))


def solution(mesh):
    placed = (
        P(("grp", "ctx"), None),
        P(("grp", "ctx"), None),
        P(("grp", "ctx"), None),
        P(("grp", "ctx")),
        P(("grp", "ctx"), None),
        P(),
    )
    return jax.shard_map(
        body, mesh=mesh, in_specs=placed, out_specs=P(("grp", "ctx"), None), check_vma=False
    )
```

time: 182 us -> 42.5 us (0.23)
  matrix products: 53.9 us -> 0 us
  Pallas kernels: 0 us -> 39.2 us
  waiting for transfers between devices: 36.4 us -> 0 us
  other arithmetic: 32.4 us -> 0 us
  local copies, waits for them, and re-layouts: 33.4 us -> 3.16 us
  starting transfers between devices: 14.7 us -> 0 us
  between operations: 10.2 us -> 0.01 us
    dot_general x8 -> x0, matrix products: 53.9 us -> none  [the longest x1 22.7 us: local_mix(): jnp.einsum('hts,shd->thd', weighted, v_heads, preferred_element_type=jnp....]
    pallas_call x0 -> x1, Pallas kernels: none -> 39.2 us  [body(): pl.pallas_call(functools.partial(kernel, n), out_shape=jax.ShapeDtypeStru...]
    ppermute x9 -> x0, waiting for transfers between devices: 36.4 us -> none  [partner(): return lax.ppermute(value, axis, pairs)]
    ppermute x9 -> x0, starting transfers between devices: 14.7 us -> none  [partner(): return lax.ppermute(value, axis, pairs)]
    select_n x6 -> x0, other arithmetic: 12.9 us -> none  [the longest x2 6.24 us: run_summary(): kept = jnp.where(keep[:, None], key, jnp.zeros_like(key))]
    slice x12 -> x0, local copies, waits for them, and re-layouts: 8.37 us -> none  [the longest x6 3.78 us: apply_level(): return (far, (merged, jnp.stack([low_meta[0], high_meta[1], single])))]
    reshape x2 -> x0, local copies, waits for them, and re-layouts: 7.89 us -> none  [run_summary(): kept.reshape(rows, H, DK)]
    unnamed x17 -> x1, local copies, waits for them, and re-layouts: 9.06 us -> 3.16 us
  transfers between devices with their start and end apart: 9 -> 0, of which waited for: 4 -> 0; matrix products, arithmetic and copies ran while one was open for 55% -> 0% of each run, Pallas kernels for 0% -> 0%
where the time goes in v1:
time: 42.5 us; the launch traced here: 42.4 us
  Pallas kernels  39.2 us (92%)
  local copies, waits for them, and re-layouts  3.16 us (7%)
    pallas_call x1, Pallas kernels, body(): pl.pallas_call(functools.partial(kernel, n), out_shape=jax.ShapeDtypeStru...  39.2 us
    unnamed x1, local copies, waits for them, and re-layouts  3.16 us

profile of v1, /device:TPU:0, one launch (start us, length us, event | category | flops | bytes accessed | tf_op | source)
XLA Modules:
  0.0 42.4 jit_solution(4283931244399133301)
XLA Ops:
  0.0 39.2 %shard_map.64 = bf16[512,2048]{1,0:T(8,128)(2,1)} custom-call(bf16[512,2048]{1,0:T(8,128)(2,1)} %q_hbm.1, bf16[512,2048]{1,0:T(8,128)(2,1)} %k_hbm.1, bf16[512,2048]{1,0:T(8,128)(2,1)} %v_hbm.1, s32[4,128]{1,0:T(4,128)} %bitcast.3, bf16[512,256]{1,0:T(8,128)(2,1)} %g_ref.1, f32[1,2048]{1,0:T(1,128)} %bitcast.2), custom_call_target="tpu_custom_call" | custom-call | tf_op jit(solution)/shard_map/pallas_call | solution.py:273
  39.2 3.2 %copy.8 = bf16[512,2048]{1,0:T(8,128)(2,1)} copy(bf16[512,2048]{1,0:T(8,128)(2,1)} %shard_map.64) | data formatting | bytes 4194304

commit v2 on v1

--- a/solution.py
+++ b/solution.py
@@ -16,7 +16,7 @@
 NC = H // HC
 HALF = NC // 2
 CW = HC * DK
-SR = CW + 16
+HOP = 4
 F32 = jnp.float32
 BF16 = jnp.bfloat16
 R2 = 2.0**-0.5
@@ -24,14 +24,20 @@
 
 
 def kernel(n, q_hbm, k_hbm, v_hbm, doc_ref, g_ref, gain_ref, out_hbm,
-           q, k, v, ost, acc, glo, gm, doct, smask, kmask, loc, mine, sbuf, rbuf,
-           ksem, vsem, qsem, osem, send_sem, recv_sem, fwd_sem):
+           q, k, v, ost, acc, glo, gm, doct, smask, kmask, loc, mine, coef, sbuf, rbuf,
+           smeta, rmeta, ksem, vsem, qsem, osem, send_sem, recv_sem, fwd_sem, msend_sem, mrecv_sem):
     nb = n.bit_length() - 1
     rows = q.shape[0]
     tiles = rows // T
     me = lax.axis_index("ctx")
     p = lax.rem(me, 2)
     sib = me + 1 - 2 * p
+    top = nb - 1
+    half = n // 2
+    above = me >= half
+    relay = above & (me + HOP < n)
+    source = (me >= half - HOP) & (me < half)
+    feeds = jnp.where((me >= half - HOP) & (me + HOP < n), 1, 0)
 
     def partner(b):
         bit = lax.rem(lax.div(me, 2**b), 2)
@@ -62,8 +68,17 @@
         load(q_hbm, q, qsem, order(i)).start()
 
     barrier = pltpu.get_barrier_semaphore()
-    for b in range(nb):
+    for b in range(top):
         pl.semaphore_signal(barrier, inc=1, device_id={"ctx": partner(b)}, device_id_type=MESH)
+
+    @pl.when(above)
+    def _():
+        pl.semaphore_signal(barrier, inc=1, device_id={"ctx": me - HOP}, device_id_type=MESH)
+
+    @pl.when(jnp.logical_not(above))
+    def _():
+        rbuf[top] = jnp.zeros_like(rbuf[top])
+        rmeta[top] = jnp.zeros_like(rmeta[top])
 
     it = lax.broadcasted_iota(jnp.int32, (T, T), 0)
     js = lax.broadcasted_iota(jnp.int32, (T, T), 1)
@@ -101,22 +116,35 @@
     def meta(first, last):
         return jnp.where(rowid == 0, first, last).astype(BF16)
 
-    meta0 = meta(firsts[0], lasts[3])
-
-    pl.semaphore_wait(barrier, nb)
+    smeta[0] = meta(firsts[0], lasts[3])
+
+    pl.semaphore_wait(barrier, top + feeds)
+
+    def target(b):
+        return sib if b == 0 else partner(b) if b < top else lax.rem(me + HOP, n)
+
+    def remote(src, b, c, sem, to):
+        return pltpu.make_async_remote_copy(
+            src_ref=src.at[b, c], dst_ref=rbuf.at[b, c],
+            send_sem=sem.at[b, c], recv_sem=recv_sem.at[b, c],
+            device_id={"ctx": to}, device_id_type=MESH)
 
     def send(b, c):
-        to = sib if b == 0 else partner(b)
+        return remote(sbuf, b, c, send_sem, target(b))
+
+    def pass_on(c):
+        return remote(rbuf, top, c, send_sem, target(top))
+
+    def forward(b, c):
+        return remote(rbuf, b, c, fwd_sem, sib)
+
+    def send_meta(b, src=smeta):
         return pltpu.make_async_remote_copy(
-            src_ref=sbuf.at[b, c], dst_ref=rbuf.at[b, c],
-            send_sem=send_sem.at[b, c], recv_sem=recv_sem.at[b, c],
-            device_id={"ctx": to}, device_id_type=MESH)
-
-    def forward(b, c):
-        return pltpu.make_async_remote_copy(
-            src_ref=rbuf.at[b, c], dst_ref=rbuf.at[b, c],
-            send_sem=fwd_sem.at[b, c], recv_sem=recv_sem.at[b, c],
-            device_id={"ctx": sib}, device_id_type=MESH)
+            src_ref=src.at[b], dst_ref=rmeta.at[b],
+            send_sem=msend_sem.at[b], recv_sem=mrecv_sem.at[b],
+            device_id={"ctx": target(b)}, device_id_type=MESH)
+
+    send_meta(0).start()
 
     def states(i, own):
         c = order(i)
@@ -139,7 +167,6 @@
             if own:
                 mine[i - HALF, x * DK : (x + 1) * DK, :] = run
             sbuf[0, c, x * DK : (x + 1) * DK, :] = run.astype(BF16)
-        sbuf[0, c, CW:SR, :] = meta0
         send(0, c).start()
 
     @pl.loop(0, HALF)
@@ -149,24 +176,39 @@
     @pl.loop(HALF, NC)
     def _(i):
         states(i, True)
+
+    def merge_meta(b):
+        send_meta(b).wait_recv()
+        up = upper(b)
+        mf, of = smeta[b].astype(F32), rmeta[b].astype(F32)
+        hi, lo = jnp.where(up, mf, of), jnp.where(up, of, mf)
+        join = joins(hi[0:1], hi[1:2], lo[1:2])
+        coef[b, 0:1, :] = jnp.where(up, 1.0, join) * R2
+        coef[b, 1:2, :] = jnp.where(up, join, 1.0) * R2
+        smeta[b + 1] = meta(lo[0:1], hi[1:2])
+        if b + 1 < top:
+            send_meta(b + 1).start()
+        else:
+
+            @pl.when(source)
+            def _():
+                send_meta(top).start()
 
     def step(b, i):
         c = p * HALF + i
         send(b, c).wait_recv()
         if b >= 1:
             forward(b, c).start()
-        if b < nb - 1:
-            up = upper(b)
-            mf = sbuf[b, c, CW:SR, :].astype(F32)
-            of = rbuf[b, c, CW:SR, :].astype(F32)
-            hi, lo = jnp.where(up, mf, of), jnp.where(up, of, mf)
-            join = joins(hi[0:1], hi[1:2], lo[1:2])
-            cm, co = jnp.where(up, 1.0, join) * R2, jnp.where(up, join, 1.0) * R2
-            merged = mine[i] * cm + rbuf[b, c, 0:CW, :].astype(F32) * co
-            mine[i] = merged
-            sbuf[b + 1, c, 0:CW, :] = merged.astype(BF16)
-            sbuf[b + 1, c, CW:SR, :] = meta(lo[0:1], hi[1:2])
+        merged = mine[i] * coef[b, 0:1, :] + rbuf[b, c].astype(F32) * coef[b, 1:2, :]
+        mine[i] = merged
+        sbuf[b + 1, c] = merged.astype(BF16)
+        if b + 1 < top:
             send(b + 1, c).start()
+        else:
+
+            @pl.when(source)
+            def _():
+                send(top, c).start()
 
     lev16 = lev * 16
 
@@ -175,6 +217,7 @@
         for x in range(HC):
             h = c * HC + x
             idx = lev16 + h
+            wide = jnp.dot(q[2 * T : 4 * T, hcols(h)], loc[2, h], preferred_element_type=F32)
             for j in range(tiles):
                 rs = slice(j * T, (j + 1) * T)
                 qj = q[rs, hcols(h)]
@@ -187,26 +230,31 @@
                     w8 = jnp.take_along_axis(gm[0, rs, :], jnp.full((T, T), h, jnp.int32), axis=1)
                     o = o + w8 * jnp.dot(qj, loc[j // 2, h], preferred_element_type=F32)
                 if j >= 2:
+                    js_ = slice((j - 2) * T, (j - 1) * T)
                     w9 = jnp.take_along_axis(gm[1, rs, :], jnp.full((T, T), 16 + h, jnp.int32), axis=1)
-                    o = o + w9 * jnp.dot(qj, loc[2, h], preferred_element_type=F32)
+                    o = o + w9 * wide[js_, :]
                 acc[rs, hcols(h)] = o
 
     def weights(b):
-        last = rbuf[b, p * HALF, CW:SR, :].astype(F32)[1:2]
-        last = jnp.where(upper(b), last, -1.0)
+        last = jnp.where(upper(b), rmeta[b].astype(F32)[1:2], -1.0)
         for j in range(tiles):
             rs = slice(j * T, (j + 1) * T)
-            gm[b % 2, rs, :] = jnp.where(doct[rs, :] == last, g_ref[rs, 128:256].astype(F32), 0.0)
-
-    def far(b, c, final):
+            gm[2 + b, rs, :] = jnp.where(doct[rs, :] == last, g_ref[rs, 128:256].astype(F32), 0.0)
+
+    def far(b, c):
+        final = b + 1 == top
         for x in range(HC):
             h = c * HC + x
-            idx = jnp.full((T, T), (2 + b) * 16 + h, jnp.int32)
-            st = rbuf[b, c, x * DK : (x + 1) * DK, :]
+            hs = slice(x * DK, (x + 1) * DK)
+            st = jnp.concatenate([rbuf[b, c, hs, :], rbuf[b + 1, c, hs, :]], axis=1)
+            m = jnp.dot(q[:, hcols(h)], st, preferred_element_type=F32)
+            i0 = jnp.full((T, T), (2 + b) * 16 + h, jnp.int32)
+            i1 = i0 + 16
             for j in range(tiles):
                 rs = slice(j * T, (j + 1) * T)
-                w = jnp.take_along_axis(gm[b % 2, rs, :], idx, axis=1)
-                a = acc[rs, hcols(h)] + w * jnp.dot(q[rs, hcols(h)], st, preferred_element_type=F32)
+                w0 = jnp.take_along_axis(gm[2 + b, rs, :], i0, axis=1)
+                w1 = jnp.take_along_axis(gm[3 + b, rs, :], i1, axis=1)
+                a = acc[rs, hcols(h)] + w0 * m[rs, 0:DK] + w1 * m[rs, DK : 2 * DK]
                 if not final:
                     acc[rs, hcols(h)] = a
                 else:
@@ -215,52 +263,117 @@
                     y = a * lax.rsqrt(ms + 1e-6) * gain_ref[:, hcols(h)]
                     ost[rs, hcols(h)] = y.astype(BF16)
 
+    def put(c):
+        return pltpu.make_async_copy(ost.at[:, cols(c)], out_hbm.at[:, cols(c)], osem.at[c])
+
+    merge_meta(0)
+
     @pl.loop(0, HALF)
     def _(i):
         step(0, i)
+
+    weights(0)
+    merge_meta(1)
+
+    @pl.loop(0, HALF)
+    def _(i):
         near(p * HALF + i)
         near((1 - p) * HALF + i)
-
-    for b in range(1, nb):
-        weights(b - 1)
+        step(1, i)
+
+    weights(1)
+    for b in range(2, top):
+        merge_meta(b)
 
         @pl.loop(0, HALF)
         def _(i):
             step(b, i)
-            far(b - 1, p * HALF + i, False)
-            oc = (1 - p) * HALF + i
-            send(b - 1, oc).wait_recv()
-            far(b - 1, oc, False)
-
-    weights(nb - 1)
-
-    def put(c):
-        return pltpu.make_async_copy(ost.at[:, cols(c)], out_hbm.at[:, cols(c)], osem.at[c])
-
-    @pl.loop(0, HALF)
-    def _(i):
-        c = p * HALF + i
-        far(nb - 1, c, True)
-        put(c).start()
-
-    @pl.loop(0, HALF)
-    def _(i):
-        c = (1 - p) * HALF + i
-        send(nb - 1, c).wait_recv()
-        far(nb - 1, c, True)
-        put(c).start()
+            if b % 2 == 0:
+                oc = (1 - p) * HALF + i
+                if b == 2:
+                    send(0, oc).wait_recv()
+                far(b - 2, p * HALF + i)
+                send(b - 1, oc).wait_recv()
+                far(b - 2, oc)
+            else:
+                send(b - 1, (1 - p) * HALF + i).wait_recv()
+
+        weights(b)
+
+    @pl.when(above)
+    def _():
+        send_meta(top).wait_recv()
+
+    @pl.when(relay)
+    def _():
+        send_meta(top, rmeta).start()
+
+        @pl.loop(0, HALF)
+        def _(i):
+            c = p * HALF + i
+            send(top, c).wait_recv()
+            pass_on(c).start()
+            forward(top, c).start()
+
+    weights(top)
+
+    def rest(i):
+        oc = (1 - p) * HALF + i
+        send(top - 1, oc).wait_recv()
+
+        @pl.when(above)
+        def _():
+            send(top, oc).wait_recv()
+
+        far(top - 1, oc)
+        put(oc).start()
+
+    @pl.loop(0, HALF + 1)
+    def _(i):
+        @pl.when(i < HALF)
+        def _():
+            c = p * HALF + i
+
+            @pl.when(above & jnp.logical_not(relay))
+            def _():
+                send(top, c).wait_recv()
+                forward(top, c).start()
+
+            far(top - 1, c)
+            put(c).start()
+
+        @pl.when(i > 0)
+        def _():
+            rest(i - 1)
 
     @pl.loop(0, NC)
     def _(i):
         send(0, i).wait_send()
         put(i).wait()
 
-    for b in range(1, nb):
+    for b in range(top):
+        send_meta(b).wait_send()
+
+    for b in range(1, top):
 
         @pl.loop(0, HALF)
         def _(i):
             send(b, p * HALF + i).wait_send()
             forward(b, p * HALF + i).wait_send()
+
+    @pl.when(feeds == 1)
+    def _():
+        send_meta(top).wait_send()
+
+        @pl.loop(0, HALF)
+        def _(i):
+            send(top, p * HALF + i).wait_send()
+
+    @pl.when(above)
+    def _():
+        @pl.loop(0, HALF)
+        def _(i):
+            forward(top, p * HALF + i).wait_send()
 
 
 def body(query, key, value, doc_ids, gates, gain):
@@ -282,16 +395,19 @@
             pltpu.VMEM((rows, width), BF16),
             pltpu.VMEM((rows, width), F32),
             pltpu.VMEM((rows, 128), F32),
-            pltpu.VMEM((2, rows, 128), F32),
+            pltpu.VMEM((2 + nb, rows, 128), F32),
             pltpu.VMEM((rows, 128), F32),
             pltpu.VMEM((rows, 128), F32),
             pltpu.VMEM((rows, 128), BF16),
             pltpu.VMEM((3, H, DK, DK), BF16),
             pltpu.VMEM((HALF, CW, DK), F32),
-            pltpu.VMEM((nb, NC, SR, DK), BF16),
-            pltpu.VMEM((nb, NC, SR, DK), BF16),
+            pltpu.VMEM((nb, 8, DK), F32),
+            pltpu.VMEM((nb, NC, CW, DK), BF16),
+            pltpu.VMEM((nb, NC, CW, DK), BF16),
+            pltpu.VMEM((nb, 16, DK), BF16),
+            pltpu.VMEM((nb, 16, DK), BF16),
             dma((NC,)), dma((NC,)), dma((NC,)), dma((NC,)),
-            dma((nb, NC)), dma((nb, NC)), dma((nb, NC)),
+            dma((nb, NC)), dma((nb, NC)), dma((nb, NC)), dma((nb,)), dma((nb,)),
         ],
         compiler_params=pltpu.CompilerParams(
             collective_id=0, has_side_effects=True, vmem_limit_bytes=56 * 2**20),

time: 42.5 us -> 34.4 us (0.81)
  the two profiles are of different devices: /device:TPU:0 before, /device:TPU:25 now
where the time goes in v2:
time: 34.4 us; the launch traced here: 34.2 us
  Pallas kernels  31.1 us (90%)
  local copies, waits for them, and re-layouts  3.16 us (9%)
    pallas_call x1, Pallas kernels, body(): pl.pallas_call(functools.partial(kernel, n), out_shape=jax.ShapeDtypeStru...  31.1 us
    unnamed x1, local copies, waits for them, and re-layouts  3.16 us

profile of v2, /device:TPU:25, one launch (start us, length us, event | category | flops | bytes accessed | tf_op | source)
XLA Modules:
  0.0 34.2 jit_solution(5470799200475037245)
XLA Ops:
  0.0 31.1 %shard_map.64 = bf16[512,2048]{1,0:T(8,128)(2,1)} custom-call(bf16[512,2048]{1,0:T(8,128)(2,1)} %q_hbm.1, bf16[512,2048]{1,0:T(8,128)(2,1)} %k_hbm.1, bf16[512,2048]{1,0:T(8,128)(2,1)} %v_hbm.1, s32[4,128]{1,0:T(4,128)} %bitcast.3, bf16[512,256]{1,0:T(8,128)(2,1)} %g_ref.1, f32[1,2048]{1,0:T(1,128)} %bitcast.2), custom_call_target="tpu_custom_call" | custom-call | tf_op jit(solution)/shard_map/pallas_call | solution.py:386
  31.1 3.2 %copy.8 = bf16[512,2048]{1,0:T(8,128)(2,1)} copy(bf16[512,2048]{1,0:T(8,128)(2,1)} %shard_map.64) | data formatting | bytes 4194304

commit v3 on v2

--- a/solution.py
+++ b/solution.py
@@ -23,9 +23,9 @@
 MESH = pl.DeviceIdType.MESH
 
 
-def kernel(n, q_hbm, k_hbm, v_hbm, doc_ref, g_ref, gain_ref, out_hbm,
-           q, k, v, ost, acc, glo, gm, doct, smask, kmask, loc, mine, coef, sbuf, rbuf,
-           smeta, rmeta, ksem, vsem, qsem, osem, send_sem, recv_sem, fwd_sem, msend_sem, mrecv_sem):
+def kernel(n, q_hbm, k_hbm, v_hbm, doc_ref, g_ref, gain_ref, ost,
+           q, k, v, acc, glo, gm, doct, smask, kmask, loc, mine, coef, sbuf, rbuf,
+           smeta, rmeta, ksem, vsem, qsem, send_sem, recv_sem, fwd_sem, msend_sem, mrecv_sem):
     nb = n.bit_length() - 1
     rows = q.shape[0]
     tiles = rows // T
@@ -263,9 +263,6 @@
                     y = a * lax.rsqrt(ms + 1e-6) * gain_ref[:, hcols(h)]
                     ost[rs, hcols(h)] = y.astype(BF16)
 
-    def put(c):
-        return pltpu.make_async_copy(ost.at[:, cols(c)], out_hbm.at[:, cols(c)], osem.at[c])
-
     merge_meta(0)
 
     @pl.loop(0, HALF)
@@ -326,7 +323,6 @@
             send(top, oc).wait_recv()
 
         far(top - 1, oc)
-        put(oc).start()
 
     @pl.loop(0, HALF + 1)
     def _(i):
@@ -340,7 +336,6 @@
                 forward(top, c).start()
 
             far(top - 1, c)
-            put(c).start()
 
         @pl.when(i > 0)
         def _():
@@ -349,7 +344,6 @@
     @pl.loop(0, NC)
     def _(i):
         send(0, i).wait_send()
-        put(i).wait()
 
     for b in range(top):
         send_meta(b).wait_send()
@@ -380,16 +374,15 @@
     n = lax.axis_size("ctx")
     nb = n.bit_length() - 1
     rows, width = query.shape
-    hbm = pl.BlockSpec(memory_space=pl.ANY)
+    hbm = pl.BlockSpec(memory_space=pltpu.HBM)
     vmem = pl.BlockSpec(memory_space=pltpu.VMEM)
     dma = pltpu.SemaphoreType.DMA
     return pl.pallas_call(
         functools.partial(kernel, n),
-        out_shape=jax.ShapeDtypeStruct((rows, width), BF16),
+        out_shape=pltpu.VMEM((rows, width), BF16),
         in_specs=[hbm, hbm, hbm, vmem, vmem, vmem],
-        out_specs=hbm,
+        out_specs=vmem,
         scratch_shapes=[
-            pltpu.VMEM((rows, width), BF16),
             pltpu.VMEM((rows, width), BF16),
             pltpu.VMEM((rows, width), BF16),
             pltpu.VMEM((rows, width), BF16),
@@ -406,11 +399,11 @@
             pltpu.VMEM((nb, NC, CW, DK), BF16),
             pltpu.VMEM((nb, 16, DK), BF16),
             pltpu.VMEM((nb, 16, DK), BF16),
-            dma((NC,)), dma((NC,)), dma((NC,)), dma((NC,)),
+            dma((NC,)), dma((NC,)), dma((NC,)),
             dma((nb, NC)), dma((nb, NC)), dma((nb, NC)), dma((nb,)), dma((nb,)),
         ],
         compiler_params=pltpu.CompilerParams(
-            collective_id=0, has_side_effects=True, vmem_limit_bytes=56 * 2**20),
+            collective_id=0, has_side_effects=True, vmem_limit_bytes=58 * 2**20),
     )(query, key, value, doc_ids.reshape(rows // T, T), gates, gain.reshape(1, width))
 
 

time: 34.4 us -> 31.8 us (0.924)
  local copies, waits for them, and re-layouts: 3.16 us -> 1.32 us
  Pallas kernels: 31.1 us -> 30.3 us
    unnamed x1, local copies, waits for them, and re-layouts: 3.16 us -> 1.32 us
    pallas_call x1, Pallas kernels: 31.1 us -> 30.3 us  [body(): pl.pallas_call(functools.partial(kernel, n), out_shape=pltpu.VMEM((rows,...]
where the time goes in v3:
time: 31.8 us; the launch traced here: 31.7 us
  Pallas kernels  30.3 us (95%)
  local copies, waits for them, and re-layouts  1.32 us (4%)
    pallas_call x1, Pallas kernels, body(): pl.pallas_call(functools.partial(kernel, n), out_shape=pltpu.VMEM((rows,...  30.3 us
    unnamed x1, local copies, waits for them, and re-layouts  1.32 us

profile of v3, /device:TPU:25, one launch (start us, length us, event | category | flops | bytes accessed | tf_op | source)
XLA Modules:
  0.0 31.7 jit_solution(7377348994389494942)
XLA Ops:
  0.0 30.3 %shard_map.64 = bf16[512,2048]{1,0:T(8,128)(2,1)S(1)} custom-call(bf16[512,2048]{1,0:T(8,128)(2,1)} %q_hbm.1, bf16[512,2048]{1,0:T(8,128)(2,1)} %k_hbm.1, bf16[512,2048]{1,0:T(8,128)(2,1)} %v_hbm.1, s32[4,128]{1,0:T(4,128)} %bitcast.3, bf16[512,256]{1,0:T(8,128)(2,1)} %g_ref.1, f32[1,2048]{1,0:T(1,128)} %bitcast.2), custom_call_target="tpu_custom_call" | custom-call | tf_op jit(solution)/shard_map/pallas_call | solution.py:380
  30.3 1.3 %copy.8 = bf16[512,2048]{1,0:T(8,128)(2,1)} copy(bf16[512,2048]{1,0:T(8,128)(2,1)S(1)} %shard_map.64) | data formatting | bytes 4194304

commit v4 on v3

--- a/solution.py
+++ b/solution.py
@@ -173,10 +173,6 @@
     def _(i):
         states(i, False)
 
-    @pl.loop(HALF, NC)
-    def _(i):
-        states(i, True)
-
     def merge_meta(b):
         send_meta(b).wait_recv()
         up = upper(b)
@@ -267,6 +263,7 @@
 
     @pl.loop(0, HALF)
     def _(i):
+        states(i + HALF, True)
         step(0, i)
 
     weights(0)

time: 31.8 us -> 30.5 us (0.959)
  Pallas kernels: 30.3 us -> 29 us
    pallas_call x1, Pallas kernels: 30.3 us -> 29 us  [body(): pl.pallas_call(functools.partial(kernel, n), out_shape=pltpu.VMEM((rows,...]
where the time goes in v4:
time: 30.5 us; the launch traced here: 30.4 us
  Pallas kernels  29 us (95%)
  local copies, waits for them, and re-layouts  1.32 us (4%)
    pallas_call x1, Pallas kernels, body(): pl.pallas_call(functools.partial(kernel, n), out_shape=pltpu.VMEM((rows,...  29 us
    unnamed x1, local copies, waits for them, and re-layouts  1.32 us

profile of v4, /device:TPU:25, one launch (start us, length us, event | category | flops | bytes accessed | tf_op | source)
XLA Modules:
  0.0 30.4 jit_solution(7865272954256306269)
XLA Ops:
  0.0 29.0 %shard_map.64 = bf16[512,2048]{1,0:T(8,128)(2,1)S(1)} custom-call(bf16[512,2048]{1,0:T(8,128)(2,1)} %q_hbm.1, bf16[512,2048]{1,0:T(8,128)(2,1)} %k_hbm.1, bf16[512,2048]{1,0:T(8,128)(2,1)} %v_hbm.1, s32[4,128]{1,0:T(4,128)} %bitcast.3, bf16[512,256]{1,0:T(8,128)(2,1)} %g_ref.1, f32[1,2048]{1,0:T(1,128)} %bitcast.2), custom_call_target="tpu_custom_call" | custom-call | tf_op jit(solution)/shard_map/pallas_call | solution.py:377
  29.0 1.3 %copy.8 = bf16[512,2048]{1,0:T(8,128)(2,1)} copy(bf16[512,2048]{1,0:T(8,128)(2,1)S(1)} %shard_map.64) | data formatting | bytes 4194304
